TPU v7x, 32 devices: a whole 2x2x4 slice. The times are simulated.
32 devices in a mesh: groups: 2 (over y), flat: 4 (over z), dp: 4 (over x, core).
Axes of the slice: x: 2, y: 2, z: 4, core: 2. Of those that a mesh axis runs over, the one named last changes fastest.
Arguments:
- activations: bfloat16 [4096, 14336], P(('groups', 'dp'), 'flat'), parts along dimension 0
- curvature: float32 [4096], P(('groups', 'dp')), parts along dimension 0, may hold values from 0.3 to 3
- vector_now: float32 [28672, 4096], P(('groups', 'flat', 'dp')), parts along dimension 0
- vector_before: float32 [28672, 4096], P(('groups', 'flat', 'dp')), parts along dimension 0, may hold values from -6 to 6
- sign_bits: int32 [28672, 4096], P(('groups', 'flat', 'dp')), parts along dimension 0, may hold values from 0 to 1
- prior_precision: float32 [2], P('groups'), parts along dimension 0, may hold values from 0.2 to 2
- beta_before: float32 [2], P('groups'), parts along dimension 0, may hold values from 0.3 to 1.5
- kept_rows: int32 [8192], P('groups'), parts along dimension 0, may hold values from 0 to 3583
- kept_cols: int32 [8192], P('groups'), parts along dimension 0, may hold values from 0 to 16383
Outputs:
- vector_next: float32 [28672, 4096], P(('groups', 'flat', 'dp')), parts along dimension 0
- alpha_value: float32 [2], P('groups'), parts along dimension 0
- beta_value: float32 [2], P('groups'), parts along dimension 0
- sketch: float32 [8192], P('groups'), parts along dimension 0
There are 2 independent parts, one for each index of `groups`. A program takes and returns all parts, laid end to end along the dimension named above; each array names one. Nothing has to cross between parts.
All inputs are finite; a program needn't handle non-finite values.
Results may differ from a plain program's by a relative error of at most 0.015.
Values may be sent and summed in bfloat16 or wider, within the bound.
A program may use at most 256 MiB of HBM per device.

v0:
```python
import math
import jax
import jax.numpy as jnp
from jax import lax
from jax.sharding import PartitionSpec as P

BLOCK = 128


def parity_sign(row_index, col_index):
    common_bits = jnp.bitwise_and(row_index, col_index)
    parity_sum = jnp.zeros_like(common_bits)
    for position in range(BLOCK.bit_length() - 1):
        parity_sum = parity_sum + jnp.bitwise_and(jnp.right_shift(common_bits, position), 1)
    return (1 - 2 * jnp.bitwise_and(parity_sum, 1)).astype(jnp.float32) / math.sqrt(BLOCK)


def hadamard_table():
    row_index = lax.broadcasted_iota(jnp.int32, (BLOCK, BLOCK), 0)
    col_index = lax.broadcasted_iota(jnp.int32, (BLOCK, BLOCK), 1)
    return parity_sign(row_index, col_index)


def pick_dense(column_block, hadamard, own_index, kept_rows, kept_cols):
    cols_here = column_block.shape[1]
    section_two = jnp.einsum(
        "ri,bic->brc",
        hadamard,
        column_block.reshape(-1, BLOCK, cols_here),
        precision=lax.Precision.HIGHEST,
    )
    section_two = section_two.reshape(-1, cols_here)
    first_col = own_index * cols_here
    inside = jnp.logical_and(kept_cols >= first_col, kept_cols < first_col + cols_here)
    local_col = jnp.clip(kept_cols - first_col, 0, cols_here - 1)
    return jnp.where(inside, section_two[kept_rows, local_col], 0.0)


def on_device(
    activations,
    curvature,
    vector_now,
    vector_before,
    sign_bits,
    prior_precision,
    beta_before,
    kept_rows,
    kept_cols,
):
    token_count = activations.shape[0]
    out_width = vector_now.shape[1]
    local_rows = vector_now.shape[0]
    flat_count = lax.axis_size("flat")
    data_count = lax.axis_size("dp")
    total_tokens = token_count * data_count
    total_cells = local_rows * out_width * flat_count * data_count
    vector_half = vector_now.astype(jnp.bfloat16)
    columns = activations
    partial_out = jnp.dot(
        columns,
        lax.all_gather(vector_half, "dp", axis=0, tiled=True),
        preferred_element_type=jnp.float32,
    )
    shares = lax.psum_scatter(
        partial_out.astype(jnp.bfloat16), "flat", scatter_dimension=1, tiled=True
    ).astype(jnp.float32)
    scaled_share = (curvature[:, None] * shares / total_tokens).astype(jnp.bfloat16)
    scaled = lax.all_gather(scaled_share, "flat", axis=1, tiled=True)
    columns = activations
    image_data = lax.psum_scatter(
        lax.dot_general(
            columns, scaled, (((0,), (0,)), ((), ())), preferred_element_type=jnp.float32
        ).astype(jnp.bfloat16),
        "dp",
        scatter_dimension=0,
        tiled=True,
    ).astype(jnp.float32)
    new_image = image_data + prior_precision[0] * vector_now
    beta_old = beta_before[0]
    alpha_value = lax.psum(jnp.sum(new_image * vector_now), ("flat", "dp")) / total_cells
    residual = new_image - alpha_value * vector_now - beta_old * vector_before
    square = lax.psum(jnp.sum(residual * residual), ("flat", "dp")) / total_cells
    beta_value = jnp.sqrt(square + 1e-06)
    vector_next = residual / beta_value
    hadamard = hadamard_table()
    signed = (2 * sign_bits - 1).astype(jnp.float32) * vector_next
    rows_here = local_rows * out_width // (BLOCK * BLOCK)
    section_one = jnp.dot(signed.reshape(-1, BLOCK), hadamard, precision=lax.Precision.HIGHEST)
    section_one = section_one.reshape(rows_here, BLOCK * BLOCK)
    own_index = lax.axis_index(("flat", "dp"))
    column_block = lax.all_to_all(
        section_one.astype(jnp.bfloat16), ("flat", "dp"), split_axis=1, concat_axis=0, tiled=True
    ).astype(section_one.dtype)
    local_values = pick_dense(column_block, hadamard, own_index, kept_rows, kept_cols)
    sketch = lax.psum(local_values, ("flat", "dp"))
    return (vector_next, alpha_value.reshape(1), beta_value.reshape(1), sketch)


def solution(mesh):
    placed = (
        P(("groups", "dp"), "flat"),
        P(("groups", "dp")),
        P(("groups", "flat", "dp"), None),
        P(("groups", "flat", "dp"), None),
        P(("groups", "flat", "dp"), None),
        P("groups"),
        P("groups"),
        P("groups"),
        P("groups"),
    )
    return jax.shard_map(
        on_device,
        mesh=mesh,
        in_specs=placed,
        out_specs=(P(("groups", "flat", "dp"), None), P("groups"), P("groups"), P("groups")),
        check_vma=False,
    )
```

profile of v0, /device:TPU:0, one launch (start us, length us, event | category | flops | bytes accessed | tf_op | source)
XLA Modules:
  0.0 1159.3 jit_solution(15920801584408900253)
XLA Ops:
  16.7 180.8 %all-gather.3.cloned.1.call-done = bf16[3584,4096]{1,0:T(8,128)(2,1)} async-done(((bf16[896,4096]{1,0:T(8,128)(2,1)}), bf16[3584,4096]{1,0:T(8,128)(2,1)}) %all-gather.3.cloned.1.call-update) | async-done | bytes 29360144 | tf_op jit(solution)/shard_map/all_gather | solution.py:61
  197.4 23.0 %convolution_convert_fusion.2 = bf16[512,4096]{1,0:T(8,128)(2,1)} fusion(bf16[512,3584]{1,0:T(8,128)(2,1)} %param.9, bf16[3584,4096]{1,0:T(8,128)(2,1)} %all-gather.3.cloned.1.call-done), kind=kOutput, calls=%fused_computation.10 | convolution fusion | flops 15034482688 | bytes 37224448 | tf_op jit(solution)/shard_map/dot_general | solution.py:59
  220.5 76.9 %reduce-scatter.5.cloned.1.call-done = bf16[512,1024]{1,0:T(8,128)(2,1)} async-done(((bf16[512,4096]{1,0:T(8,128)(2,1)}), bf16[512,1024]{1,0:T(8,128)(2,1)}) %reduce-scatter.5.cloned.1.call-update) | async-done | bytes 1048592 | tf_op jit(solution)/shard_map/reduce_scatter | solution.py:64
  300.2 81.2 %all-gather.5.cloned.1.call-done = bf16[512,4096]{1,0:T(8,128)(2,1)} async-done(((bf16[512,1024]{1,0:T(8,128)(2,1)}), bf16[512,4096]{1,0:T(8,128)(2,1)}) %all-gather.5.cloned.1.call-update) | async-done | bytes 4194320 | tf_op jit(solution)/shard_map/all_gather | solution.py:68
  381.4 22.3 %fusion = bf16[3584,4096]{0,1:T(8,128)(2,1)} fusion(bf16[512,4096]{1,0:T(8,128)(2,1)} %all-gather.5.cloned.1.call-done, bf16[512,3584]{1,0:T(8,128)(2,1)} %param.9), kind=kOutput, calls=%fused_computation.3 | convolution fusion | flops 15047065600 | bytes 37224448 | tf_op jit(solution)/shard_map/dot_general | solution.py:71
  403.7 37.0 %copy.36 = bf16[3584,4096]{1,0:T(8,128)(2,1)} copy(bf16[3584,4096]{0,1:T(8,128)(2,1)} %fusion) | data formatting | bytes 58720256
  440.7 16.7 %copy.28 = f32[896,4096]{0,1:T(8,128)} copy(f32[896,4096]{1,0:T(8,128)} %param.11) | data formatting | bytes 29360128 | tf_op args[2]
  458.1 18.0 %copy.31 = f32[896,4096]{0,1:T(8,128)} copy(f32[896,4096]{1,0:T(8,128)} %param.12) | data formatting | bytes 29360128 | tf_op args[3]
  476.1 171.1 %reduce-scatter.7.cloned.1.call-done = bf16[896,4096]{1,0:T(8,128)(2,1)} async-done(((bf16[3584,4096]{1,0:T(8,128)(2,1)}), bf16[896,4096]{1,0:T(8,128)(2,1)}) %reduce-scatter.7.cloned.1.call-update) | async-done | bytes 7340048
  658.1 11.6 %multiply_reduce_fusion.1 = f32[]{:T(128)} fusion(f32[896,4096]{0,1:T(8,128)} %copy.28, bf16[896,4096]{0,1:T(8,128)(2,1)} %copy.37, f32[]{:T(128)} %bitcast.22), kind=kLoop, calls=%fused_computation.7 | loop fusion | flops 18350080 | bytes 22020104 | tf_op jit(solution)/shard_map/reduce_sum | solution.py:80
  670.4 32.9 %psum.21 = f32[]{:T(128)} all-reduce(f32[]{:T(128)} %multiply_reduce_fusion.1), channel_id=1, replica_groups=mesh['groups'=2,'flat'=4,'dp'=4] {'flat','dp'}, use_global_device_ids=true, to_apply=%region_3.0 | all-reduce | flops 1 | bytes 8 | tf_op jit(solution)/shard_map/psum | solution.py:80
  703.9 13.4 %multiply_reduce_fusion = f32[]{:T(128)} fusion(f32[896,4096]{0,1:T(8,128)} %copy.31, f32[]{:T(128)} %bitcast.25, f32[896,4096]{0,1:T(8,128)} %copy.28, f32[]{:T(128)} %div.28, f32[]{:T(128)} %bitcast.23, bf16[896,4096]{0,1:T(8,128)(2,1)} %copy.37), kind=kLoop, calls=%fused_computation.5 | loop fusion | flops 33030144 | bytes 36700176 | tf_op jit(solution)/shard_map/reduce_sum | solution.py:82
  717.3 16.1 %copy.32 = s32[896,4096]{0,1:T(8,128)} copy(s32[896,4096]{1,0:T(8,128)} %param.13) | data formatting | bytes 29360128 | tf_op args[4]
  733.4 30.3 %psum.22 = f32[]{:T(128)} all-reduce(f32[]{:T(128)} %multiply_reduce_fusion), channel_id=1, replica_groups=mesh['groups'=2,'flat'=4,'dp'=4] {'flat','dp'}, use_global_device_ids=true, to_apply=%region_5.0 | all-reduce | flops 1 | bytes 8 | tf_op jit(solution)/shard_map/psum | solution.py:82
  764.4 28.3 %convert_multiply_fusion = (f32[896,4096]{0,1:T(8,128)}, f32[896,4096]{0,1:T(8,128)}) fusion(s32[896,4096]{0,1:T(8,128)} %copy.32, f32[]{:T(128)} %sqrt.3, f32[896,4096]{0,1:T(8,128)} %copy.31, f32[]{:T(128)} %bitcast.26, f32[896,4096]{0,1:T(8,128)} %copy.28, f32[]{:T(128)} %div.28, f32[]{:T(128)} %bitcast.24, bf16[896,4096]{0,1:T(8,128)(2,1)} %copy.37), kind=kLoop, calls=%fused_computation.4 | loop fusion | flops 44040192 | bytes 80740368 | tf_op jit(solution)/shard_map/mul | solution.py:86
  792.7 16.1 %copy.33 = f32[896,4096]{1,0:T(8,128)} copy(f32[896,4096]{0,1:T(8,128)} %get-tuple-element.16) | data formatting | bytes 29360128 | tf_op jit(solution)/shard_map/mul | solution.py:86
  808.8 15.8 %reshape.33 = f32[28672,128]{1,0:T(8,128)} reshape(f32[896,4096]{1,0:T(8,128)} %copy.33) | data formatting | bytes 29360128 | tf_op jit(solution)/shard_map/reshape | solution.py:88
  824.6 15.6 %convolution_convert_fusion = bf16[28672,128]{1,0:T(8,128)(2,1)} fusion(f32[28672,128]{1,0:T(8,128)} %reshape.33), kind=kOutput, calls=%fused_computation.1 | convolution fusion | flops 5641240576 | bytes 22020096 | tf_op jit(solution)/shard_map/dot_general | solution.py:88
  840.3 11.8 %convert_element_type.47 = bf16[224,16,1024]{2,1,0:T(8,128)(2,1)} reshape(bf16[28672,128]{1,0:T(8,128)(2,1)} %convolution_convert_fusion) | data formatting | bytes 14680064 | tf_op jit(solution)/shard_map/convert_element_type | solution.py:92
  867.2 16.1 %copy.35 = f32[896,4096]{1,0:T(8,128)} copy(f32[896,4096]{0,1:T(8,128)} %get-tuple-element.17) | data formatting | bytes 29360128
  883.3 116.0 %all-to-all-done = bf16[224,16,1024]{2,0,1:T(8,128)(2,1)} async-done(((bf16[224,16,1024]{2,0,1:T(8,128)(2,1)}), bf16[224,16,1024]{2,0,1:T(8,128)(2,1)}, u32[]{:S(2)}, u32[]{:S(2)}) %all-to-all-start) | async-done | bytes 7340064 | tf_op jit(solution)/shard_map/all_to_all | solution.py:91
  999.3 12.7 %fusion.1 = f32[28,1024,128]{1,2,0:T(8,128)} fusion(bf16[28,128,1024]{2,1,0:T(8,128)(2,1)} %bitcast.6), kind=kOutput, calls=%fused_computation.12 | convolution fusion | flops 5637570560 | bytes 22020096 | tf_op jit(solution)/shard_map/ri,bic->brc/dot_general | solution.py:26
  1012.0 50.1 %gather_fusion = f32[4096]{0:T(1024)S(1)} fusion(f32[3584,1024]{1,0:T(8,128)} %bitcast.27, s32[4096]{0:T(1024)S(1)} %fusion.5), kind=kCustom, calls=%fused_computation | custom fusion | bytes 65536 | tf_op jit(solution)/shard_map/gather | solution.py:36
  1062.1 88.3 %psum.23 = f32[4096]{0:T(1024)} all-reduce(f32[4096]{0:T(1024)S(1)} %and_select_fusion), channel_id=1, replica_groups=mesh['groups'=2,'flat'=4,'dp'=4] {'flat','dp'}, use_global_device_ids=true, to_apply=%region_6.7 | all-reduce | flops 4096 | bytes 32768 | tf_op jit(solution)/shard_map/psum | solution.py:95
  (21 shorter events, 38.3 us)
Async XLA Ops:
  7.2 190.3 %all-gather.3.cloned.1.call-start = ((), (), s32[]{:S(2)}) async-start(), calls=%async_computation.3 | async-start | bytes 36700160 | tf_op jit(solution)/shard_map/all_gather | solution.py:61
  16.6 280.8 %copy-start.2 = (f32[512]{0:T(512)S(1)}, f32[512]{0:T(512)}, u32[]{:S(2)}) copy-start(f32[512]{0:T(512)} %param.10) | copy-start | bytes 6148
  16.6 280.8 %reduce-scatter.5.cloned.1.call-start = ((), (), s32[]{:S(2)}) async-start(), calls=%async_computation.4 | async-start | bytes 5242880 | tf_op jit(solution)/shard_map/reduce_scatter | solution.py:64
  220.5 160.9 %all-gather.5.cloned.1.call-start = ((), (), s32[]{:S(2)}) async-start(), calls=%async_computation.5 | async-start | bytes 5242880 | tf_op jit(solution)/shard_map/all_gather | solution.py:68
  299.9 347.3 %reduce-scatter.7.cloned.1.call-start = ((), (), s32[]{:S(2)}) async-start(), calls=%async_computation.6 | async-start | bytes 36700160
  852.0 15.2 %copy-start = (s32[4096]{0:T(1024)S(1)}, s32[4096]{0:T(1024)}, u32[]{:S(2)}) copy-start(s32[4096]{0:T(1024)} %param.17) | copy-start | bytes 49156
  852.0 15.2 %copy-start.1 = (s32[4096]{0:T(1024)S(1)}, s32[4096]{0:T(1024)}, u32[]{:S(2)}) copy-start(s32[4096]{0:T(1024)} %param.16) | copy-start | bytes 49156
  862.2 137.1 %all-to-all-start = ((bf16[224,16,1024]{2,0,1:T(8,128)(2,1)}), bf16[224,16,1024]{2,0,1:T(8,128)(2,1)}, u32[]{:S(2)}, u32[]{:S(2)}) async-start(bf16[224,16,1024]{2,0,1:T(8,128)(2,1)} %copy.34), calls=%async_computation.1 | async-start | bytes 14680064 | tf_op jit(solution)/shard_map/all_to_all | solution.py:91
Sparse Core Ops, SparseCore 0:
  16.7 180.6 all-gather.2
  220.6 76.7 reduce-scatter.4
  300.1 81.2 all-gather.4
  440.8 206.3 reduce-scatter.6
where the time goes:
time: 1160 us
  waiting for transfers between devices  626 us (54%)
  local copies, waits for them, and re-layouts  219 us (19%)
  blocking collectives  152 us (13%)
  matrix products  73.6 us (6%)
  other arithmetic  65.2 us (6%)
  between operations  18.8 us (2%)
    all_gather x1, waiting for transfers between devices, on_device(): lax.all_gather(vector_half, 'dp', axis=0, tiled=True)  181 us
    unnamed x5, waiting for transfers between devices  171 us
    all_to_all x1, waiting for transfers between devices, on_device(): lax.all_to_all(section_one.astype(jnp.bfloat16), ('flat', 'dp'), split_ax...  116 us
    unnamed x12, local copies, waits for them, and re-layouts  115 us
    psum x1, blocking collectives, on_device(): sketch = lax.psum(local_values, ('flat', 'dp'))  88.3 us
    all_gather x1, waiting for transfers between devices, on_device(): scaled = lax.all_gather(scaled_share, 'flat', axis=1, tiled=True)  81.2 us
    reduce_scatter x1, waiting for transfers between devices, on_device(): lax.psum_scatter(partial_out.astype(jnp.bfloat16), 'flat', scatter_dimens...  76.9 us
    gather x1, local copies, waits for them, and re-layouts, pick_dense(): return jnp.where(inside, section_two[kept_rows, local_col], 0.0)  50.1 us
  transfers between devices with their start and end apart: 5, of which 5 were waited for; matrix products, arithmetic and copies ran while one was open for 4% of the time, Pallas kernels for 0%

commit v1 on v0

--- a/solution.py
+++ b/solution.py
@@ -5,6 +5,29 @@
 from jax.sharding import PartitionSpec as P
 
 BLOCK = 128
+
+
+def in_blocks(shard, dim, count):
+    shape = shard.shape
+    pieces = shard.reshape(*shape[:dim], count, shape[dim] // count, *shape[dim + 1 :])
+    return jnp.moveaxis(pieces, dim, 0)
+
+
+def laid_out(pieces, dim):
+    shape = list(pieces.shape[1:])
+    shape[dim] *= pieces.shape[0]
+    return jnp.moveaxis(pieces, 0, dim).reshape(shape)
+
+
+def pairwise_exchange(x, axis, split_dim, concat_dim):
+    peers, index = (lax.axis_size(axis), lax.axis_index(axis))
+    blocks = in_blocks(x, split_dim, peers)
+    done = [blocks[index]]
+    for step in range(1, peers):
+        sent = blocks[index ^ step]
+        done.append(lax.ppermute(sent, axis, [(i, i ^ step) for i in range(peers)]))
+    blocks = jnp.stack(done)[index ^ jnp.arange(peers)]
+    return laid_out(blocks, concat_dim)
 
 
 def parity_sign(row_index, col_index):
@@ -88,9 +111,9 @@
     section_one = jnp.dot(signed.reshape(-1, BLOCK), hadamard, precision=lax.Precision.HIGHEST)
     section_one = section_one.reshape(rows_here, BLOCK * BLOCK)
     own_index = lax.axis_index(("flat", "dp"))
-    column_block = lax.all_to_all(
-        section_one.astype(jnp.bfloat16), ("flat", "dp"), split_axis=1, concat_axis=0, tiled=True
-    ).astype(section_one.dtype)
+    column_block = pairwise_exchange(section_one.astype(jnp.bfloat16), ("flat", "dp"), 1, 0).astype(
+        section_one.dtype
+    )
     local_values = pick_dense(column_block, hadamard, own_index, kept_rows, kept_cols)
     sketch = lax.psum(local_values, ("flat", "dp"))
     return (vector_next, alpha_value.reshape(1), beta_value.reshape(1), sketch)

time: 1160 us -> 1220 us (1.052); the launches traced: 1160 us -> 1210 us
  local copies, waits for them, and re-layouts: 219 us -> 286 us
  waiting for transfers between devices: 626 us -> 598 us
    all_to_all x1 -> x0, waiting for transfers between devices: 116 us -> none  [on_device(): lax.all_to_all(section_one.astype(jnp.bfloat16), ('flat', 'dp'), split_ax...]
    ppermute x0 -> x15, waiting for transfers between devices: none -> 105 us  [pairwise_exchange(): done.append(lax.ppermute(sent, axis, [(i, i ^ step) for i in range(peers)]))]
    unnamed x12 -> x60, local copies, waits for them, and re-layouts: 115 us -> 153 us
    another operation x0 -> x2, local copies, waits for them, and re-layouts: none -> 32.5 us
    unnamed x5, waiting for transfers between devices: 171 us -> 154 us
    ppermute x0 -> x15, starting transfers between devices: none -> 13.2 us  [pairwise_exchange(): done.append(lax.ppermute(sent, axis, [(i, i ^ step) for i in range(peers)]))]
  transfers between devices with their start and end apart: 5 -> 19, of which waited for: 5 -> 10; matrix products, arithmetic and copies ran while one was open for 4% -> 8% of each run, Pallas kernels for 0% -> 0%
where the time goes in v1:
time: 1220 us; the launch traced here: 1210 us
  waiting for transfers between devices  598 us (49%)
  local copies, waits for them, and re-layouts  286 us (23%)
  blocking collectives  151 us (12%)
  matrix products  73.6 us (6%)
  other arithmetic  65.3 us (5%)
  between operations  19.1 us (2%)
  starting transfers between devices  13.9 us (1%)
    all_gather x1, waiting for transfers between devices, on_device(): lax.all_gather(vector_half, 'dp', axis=0, tiled=True)  181 us
    unnamed x5, waiting for transfers between devices  154 us
    unnamed x60, local copies, waits for them, and re-layouts  153 us
    ppermute x15, waiting for transfers between devices, pairwise_exchange(): done.append(lax.ppermute(sent, axis, [(i, i ^ step) for i in range(peers)]))  105 us
    psum x1, blocking collectives, on_device(): sketch = lax.psum(local_values, ('flat', 'dp'))  87.6 us
    all_gather x1, waiting for transfers between devices, on_device(): scaled = lax.all_gather(scaled_share, 'flat', axis=1, tiled=True)  80.9 us
    reduce_scatter x1, waiting for transfers between devices, on_device(): lax.psum_scatter(partial_out.astype(jnp.bfloat16), 'flat', scatter_dimens...  76.9 us
    gather x1, local copies, waits for them, and re-layouts, pick_dense(): return jnp.where(inside, section_two[kept_rows, local_col], 0.0)  50.2 us
  transfers between devices with their start and end apart: 19, of which 10 were waited for; matrix products, arithmetic and copies ran while one was open for 8% of the time, Pallas kernels for 0%

profile of v1, /device:TPU:0, one launch (start us, length us, event | category | flops | bytes accessed | tf_op | source)
XLA Modules:
  0.0 1207.1 jit_solution(17791406460063337471)
XLA Ops:
  16.7 180.8 %all-gather.3.cloned.1.call-done = bf16[3584,4096]{1,0:T(8,128)(2,1)} async-done(((bf16[896,4096]{1,0:T(8,128)(2,1)}), bf16[3584,4096]{1,0:T(8,128)(2,1)}) %all-gather.3.cloned.1.call-update) | async-done | bytes 29360144 | tf_op jit(solution)/shard_map/all_gather | solution.py:84
  197.4 23.0 %convolution_convert_fusion.2 = bf16[512,4096]{1,0:T(8,128)(2,1)} fusion(bf16[512,3584]{1,0:T(8,128)(2,1)} %param.9, bf16[3584,4096]{1,0:T(8,128)(2,1)} %all-gather.3.cloned.1.call-done), kind=kOutput, calls=%fused_computation.11 | convolution fusion | flops 15034482688 | bytes 37224448 | tf_op jit(solution)/shard_map/dot_general | solution.py:82
  220.5 76.9 %reduce-scatter.5.cloned.1.call-done = bf16[512,1024]{1,0:T(8,128)(2,1)} async-done(((bf16[512,4096]{1,0:T(8,128)(2,1)}), bf16[512,1024]{1,0:T(8,128)(2,1)}) %reduce-scatter.5.cloned.1.call-update) | async-done | bytes 1048592 | tf_op jit(solution)/shard_map/reduce_scatter | solution.py:87
  300.4 80.9 %all-gather.5.cloned.1.call-done = bf16[512,4096]{1,0:T(8,128)(2,1)} async-done(((bf16[512,1024]{1,0:T(8,128)(2,1)}), bf16[512,4096]{1,0:T(8,128)(2,1)}) %all-gather.5.cloned.1.call-update) | async-done | bytes 4194320 | tf_op jit(solution)/shard_map/all_gather | solution.py:91
  381.4 22.3 %fusion = bf16[3584,4096]{0,1:T(8,128)(2,1)} fusion(bf16[512,4096]{1,0:T(8,128)(2,1)} %all-gather.5.cloned.1.call-done, bf16[512,3584]{1,0:T(8,128)(2,1)} %param.9), kind=kOutput, calls=%fused_computation.4 | convolution fusion | flops 15047065600 | bytes 37224448 | tf_op jit(solution)/shard_map/dot_general | solution.py:94
  403.7 39.6 %copy.65 = bf16[3584,4096]{1,0:T(8,128)(2,1)} copy(bf16[3584,4096]{0,1:T(8,128)(2,1)} %fusion) | data formatting | bytes 58720256
  443.4 16.6 %copy.42 = f32[896,4096]{0,1:T(8,128)} copy(f32[896,4096]{1,0:T(8,128)} %param.11) | data formatting | bytes 29360128 | tf_op args[2]
  460.6 18.0 %copy.45 = f32[896,4096]{0,1:T(8,128)} copy(f32[896,4096]{1,0:T(8,128)} %param.12) | data formatting | bytes 29360128 | tf_op args[3]
  479.3 16.3 %copy.46 = s32[896,4096]{0,1:T(8,128)} copy(s32[896,4096]{1,0:T(8,128)} %param.13) | data formatting | bytes 29360128 | tf_op args[4]
  495.6 154.3 %reduce-scatter.7.cloned.1.call-done = bf16[896,4096]{1,0:T(8,128)(2,1)} async-done(((bf16[3584,4096]{1,0:T(8,128)(2,1)}), bf16[896,4096]{1,0:T(8,128)(2,1)}) %reduce-scatter.7.cloned.1.call-update) | async-done | bytes 7340048
  672.3 32.9 %psum.21 = f32[]{:T(128)} all-reduce(f32[]{:T(128)} %multiply_reduce_fusion.1), channel_id=1, replica_groups=mesh['groups'=2,'flat'=4,'dp'=4] {'flat','dp'}, use_global_device_ids=true, to_apply=%region_3.0 | all-reduce | flops 1 | bytes 8 | tf_op jit(solution)/shard_map/psum | solution.py:103
  705.8 13.4 %multiply_reduce_fusion = f32[]{:T(128)} fusion(f32[896,4096]{0,1:T(8,128)} %copy.45, f32[]{:T(128)} %bitcast.104, f32[896,4096]{0,1:T(8,128)} %copy.42, f32[]{:T(128)} %div.28, f32[]{:T(128)} %bitcast.102, bf16[896,4096]{0,1:T(8,128)(2,1)} %copy.66), kind=kLoop, calls=%fused_computation.6 | loop fusion | flops 33030144 | bytes 36700176 | tf_op jit(solution)/shard_map/reduce_sum | solution.py:105
  719.2 30.3 %psum.22 = f32[]{:T(128)} all-reduce(f32[]{:T(128)} %multiply_reduce_fusion), channel_id=1, replica_groups=mesh['groups'=2,'flat'=4,'dp'=4] {'flat','dp'}, use_global_device_ids=true, to_apply=%region_5.0 | all-reduce | flops 1 | bytes 8 | tf_op jit(solution)/shard_map/psum | solution.py:105
  750.2 28.3 %convert_multiply_fusion = (f32[896,4096]{0,1:T(8,128)}, f32[896,4096]{0,1:T(8,128)}) fusion(s32[896,4096]{0,1:T(8,128)} %copy.46, f32[]{:T(128)} %sqrt.3, f32[896,4096]{0,1:T(8,128)} %copy.45, f32[]{:T(128)} %bitcast.105, f32[896,4096]{0,1:T(8,128)} %copy.42, f32[]{:T(128)} %div.28, f32[]{:T(128)} %bitcast.103, bf16[896,4096]{0,1:T(8,128)(2,1)} %copy.66), kind=kLoop, calls=%fused_computation.5 | loop fusion | flops 44040192 | bytes 80740368 | tf_op jit(solution)/shard_map/mul | solution.py:109
  778.5 16.1 %copy.47 = f32[896,4096]{1,0:T(8,128)} copy(f32[896,4096]{0,1:T(8,128)} %get-tuple-element.16) | data formatting | bytes 29360128 | tf_op jit(solution)/shard_map/mul | solution.py:109
  794.6 15.8 %reshape.79 = f32[28672,128]{1,0:T(8,128)} reshape(f32[896,4096]{1,0:T(8,128)} %copy.47) | data formatting | bytes 29360128 | tf_op jit(solution)/shard_map/reshape | solution.py:111
  810.4 15.6 %convolution_convert_fusion = bf16[28672,128]{1,0:T(8,128)(2,1)} fusion(f32[28672,128]{1,0:T(8,128)} %reshape.79), kind=kOutput, calls=%fused_computation.2 | convolution fusion | flops 5641240576 | bytes 22020096 | tf_op jit(solution)/shard_map/dot_general | solution.py:111
  837.7 31.7 %constant_dynamic-slice_fusion = (bf16[224,1,1024]{2,1,0:T(2,128)(2,1)S(1)}, bf16[224,1,1024]{2,1,0:T(2,128)(2,1)S(1)}, bf16[224,1,1024]{2,1,0:T(2,128)(2,1)S(1)...) fusion(bf16[224,16,1024]{2,1,0:T(8,128)(2,1)} %convert_element_, ...), kind=kLoop, calls=%fused_computation.58 | loop fusion | bytes 14680128 | tf_op jit(solution)/shard_map/dynamic-slice.15
  892.3 16.1 %copy.64 = f32[896,4096]{1,0:T(8,128)} copy(f32[896,4096]{0,1:T(8,128)} %get-tuple-element.17) | data formatting | bytes 29360128
  947.7 36.6 %collective-permute-done.7 = bf16[224,1024]{1,0:T(8,128)(2,1)S(1)} collective-permute-done((bf16[224,1024]{1,0:T(8,128)(2,1)}, bf16[224,1024]{1,0:T(8,128)(2,1)S(1)}, u32[]{:S(2)}, u32[]{:S(2)}) %collective-permute-start.7) | collective-permute-done | bytes 458784 | tf_op jit(solution)/shard_map/ppermute | solution.py:28
  998.6 19.9 %collective-permute-done.9 = bf16[224,1024]{1,0:T(8,128)(2,1)S(1)} collective-permute-done((bf16[224,1024]{1,0:T(8,128)(2,1)}, bf16[224,1024]{1,0:T(8,128)(2,1)S(1)}, u32[]{:S(2)}, u32[]{:S(2)}) %collective-permute-start.9) | collective-permute-done | bytes 458784 | tf_op jit(solution)/shard_map/ppermute | solution.py:28
  1019.6 16.8 %collective-permute-done.10 = bf16[224,1024]{1,0:T(8,128)(2,1)S(1)} collective-permute-done((bf16[224,1024]{1,0:T(8,128)(2,1)}, bf16[224,1024]{1,0:T(8,128)(2,1)S(1)}, u32[]{:S(2)}, u32[]{:S(2)}) %collective-permute-start.10) | collective-permute-done | bytes 458784 | tf_op jit(solution)/shard_map/ppermute | solution.py:28
  1060.2 50.2 %gather_fusion.1 = f32[4096]{0:T(1024)S(1)} fusion(f32[3584,1024]{1,0:T(8,128)} %bitcast.106, s32[4096]{0:T(1024)S(1)} %fusion.6), kind=kCustom, calls=%fused_computation.1 | custom fusion | bytes 65536 | tf_op jit(solution)/shard_map/gather | solution.py:59
  1110.5 87.6 %psum.23 = f32[4096]{0:T(1024)} all-reduce(f32[4096]{0:T(1024)S(1)} %and_select_fusion), channel_id=1, replica_groups=mesh['groups'=2,'flat'=4,'dp'=4] {'flat','dp'}, use_global_device_ids=true, to_apply=%region_6.7 | all-reduce | flops 4096 | bytes 32768 | tf_op jit(solution)/shard_map/psum | solution.py:118
  (101 shorter events, 148.0 us)
Async XLA Ops:
  7.2 190.3 %all-gather.3.cloned.1.call-start = ((), (), s32[]{:S(2)}) async-start(), calls=%async_computation.2 | async-start | bytes 36700160 | tf_op jit(solution)/shard_map/all_gather | solution.py:84
  16.6 280.8 %copy-start.11 = (f32[512]{0:T(512)S(1)}, f32[512]{0:T(512)}, u32[]{:S(2)}) copy-start(f32[512]{0:T(512)} %param.10) | copy-start | bytes 6148
  16.6 280.8 %reduce-scatter.5.cloned.1.call-start = ((), (), s32[]{:S(2)}) async-start(), calls=%async_computation.3 | async-start | bytes 5242880 | tf_op jit(solution)/shard_map/reduce_scatter | solution.py:87
  220.5 160.9 %all-gather.5.cloned.1.call-start = ((), (), s32[]{:S(2)}) async-start(), calls=%async_computation.4 | async-start | bytes 5242880 | tf_op jit(solution)/shard_map/all_gather | solution.py:91
  299.9 350.0 %reduce-scatter.7.cloned.1.call-start = ((), (), s32[]{:S(2)}) async-start(), calls=%async_computation.5 | async-start | bytes 36700160
  837.7 34.0 %copy-start.9 = (s32[4096]{0:T(1024)S(1)}, s32[4096]{0:T(1024)}, u32[]{:S(2)}) copy-start(s32[4096]{0:T(1024)} %param.17) | copy-start | bytes 49156
  837.7 34.0 %copy-start.10 = (s32[4096]{0:T(1024)S(1)}, s32[4096]{0:T(1024)}, u32[]{:S(2)}) copy-start(s32[4096]{0:T(1024)} %param.16) | copy-start | bytes 49156
  871.7 37.6 %collective-permute-start = (bf16[224,1024]{1,0:T(8,128)(2,1)}, bf16[224,1024]{1,0:T(8,128)(2,1)}, u32[]{:S(2)}, u32[]{:S(2)}) collective-permute-start(bf16[224,1024]{1,0:T(8,128)(2,1)} %bitcast.100), channel_id=1, source_target_pairs={{0,1},{1,0},{2,3},{3,2},{4,5},{5,4},{6,7},{7,6},{8,9},{9,8},{10,11... | collective-permute-start | bytes 1376264 | tf_op jit(solution)/shard_map/ppermute | solution.py:28
  873.9 37.3 %collective-permute-start.1 = (bf16[224,1024]{1,0:T(8,128)(2,1)}, bf16[224,1024]{1,0:T(8,128)(2,1)}, u32[]{:S(2)}, u32[]{:S(2)}) collective-permute-start(bf16[224,1024]{1,0:T(8,128)(2,1)} %bitcast.99), channel_id=1, source_target_pairs={{0,2},{1,3},{2,0},{3,1},{4,6},{5,7},{6,4},{7,5},{8,10},{9,11},{10,... | collective-permute-start | bytes 1376264 | tf_op jit(solution)/shard_map/ppermute | solution.py:28
  876.0 39.7 %collective-permute-start.2 = (bf16[224,1024]{1,0:T(8,128)(2,1)}, bf16[224,1024]{1,0:T(8,128)(2,1)}, u32[]{:S(2)}, u32[]{:S(2)}) collective-permute-start(bf16[224,1024]{1,0:T(8,128)(2,1)} %bitcast.98), channel_id=1, source_target_pairs={{0,3},{1,2},{2,1},{3,0},{4,7},{5,6},{6,5},{7,4},{8,11},{9,10},{10,... | collective-permute-start | bytes 1376264 | tf_op jit(solution)/shard_map/ppermute | solution.py:28
  880.0 37.6 %collective-permute-start.3 = (bf16[224,1024]{1,0:T(8,128)(2,1)}, bf16[224,1024]{1,0:T(8,128)(2,1)}, u32[]{:S(2)}, u32[]{:S(2)}) collective-permute-start(bf16[224,1024]{1,0:T(8,128)(2,1)} %bitcast.97), channel_id=1, source_target_pairs={{0,4},{1,5},{2,6},{3,7},{4,0},{5,1},{6,2},{7,3},{8,12},{9,13},{10,... | collective-permute-start | bytes 1376264 | tf_op jit(solution)/shard_map/ppermute | solution.py:28
  882.1 39.8 %collective-permute-start.4 = (bf16[224,1024]{1,0:T(8,128)(2,1)}, bf16[224,1024]{1,0:T(8,128)(2,1)S(1)}, u32[]{:S(2)}, u32[]{:S(2)}) collective-permute-start(bf16[224,1024]{1,0:T(8,128)(2,1)} %bitcast.96), channel_id=1, source_target_pairs={{0,5},{1,4},{2,7},{3,6},{4,1},{5,0},{6,3},{7,2},{8,13},{9,12},{10,... | collective-permute-start | bytes 1376264 | tf_op jit(solution)/shard_map/ppermute | solution.py:28
  908.4 75.9 %copy-start.8 = (bf16[224,1,1024]{2,0,1:T(8,128)(2,1)S(1)}, bf16[224,1,1024]{2,0,1:T(8,128)(2,1)}, u32[]{:S(2)}) copy-start(bf16[224,1,1024]{2,0,1:T(8,128)(2,1)} %copy.103) | copy-start | bytes 1376260
  908.4 89.4 %copy-start.7 = (bf16[224,1,1024]{2,0,1:T(8,128)(2,1)S(1)}, bf16[224,1,1024]{2,0,1:T(8,128)(2,1)}, u32[]{:S(2)}) copy-start(bf16[224,1,1024]{2,0,1:T(8,128)(2,1)} %copy.102) | copy-start | bytes 1376260
  909.3 25.1 %collective-permute-start.5 = (bf16[224,1024]{1,0:T(8,128)(2,1)}, bf16[224,1024]{1,0:T(8,128)(2,1)S(1)}, u32[]{:S(2)}, u32[]{:S(2)}) collective-permute-start(bf16[224,1024]{1,0:T(8,128)(2,1)} %bitcast.95), channel_id=1, source_target_pairs={{0,6},{1,7},{2,4},{3,5},{4,2},{5,3},{6,0},{7,1},{8,14},{9,15},{10,... | collective-permute-start | bytes 1376264 | tf_op jit(solution)/shard_map/ppermute | solution.py:28
  911.2 32.2 %collective-permute-start.6 = (bf16[224,1024]{1,0:T(8,128)(2,1)}, bf16[224,1024]{1,0:T(8,128)(2,1)S(1)}, u32[]{:S(2)}, u32[]{:S(2)}) collective-permute-start(bf16[224,1024]{1,0:T(8,128)(2,1)} %bitcast.94), channel_id=1, source_target_pairs={{0,7},{1,6},{2,5},{3,4},{4,3},{5,2},{6,1},{7,0},{8,15},{9,14},{10,... | collective-permute-start | bytes 1376264 | tf_op jit(solution)/shard_map/ppermute | solution.py:28
  915.7 68.6 %collective-permute-start.7 = (bf16[224,1024]{1,0:T(8,128)(2,1)}, bf16[224,1024]{1,0:T(8,128)(2,1)S(1)}, u32[]{:S(2)}, u32[]{:S(2)}) collective-permute-start(bf16[224,1024]{1,0:T(8,128)(2,1)} %bitcast.93), channel_id=1, source_target_pairs={{0,8},{1,9},{2,10},{3,11},{4,12},{5,13},{6,14},{7,15},{8,0},{9,1},... | collective-permute-start | bytes 1376264 | tf_op jit(solution)/shard_map/ppermute | solution.py:28
  917.5 80.2 %collective-permute-start.8 = (bf16[224,1024]{1,0:T(8,128)(2,1)}, bf16[224,1024]{1,0:T(8,128)(2,1)S(1)}, u32[]{:S(2)}, u32[]{:S(2)}) collective-permute-start(bf16[224,1024]{1,0:T(8,128)(2,1)} %bitcast.92), channel_id=1, source_target_pairs={{0,9},{1,8},{2,11},{3,10},{4,13},{5,12},{6,15},{7,14},{8,1},{9,0},... | collective-permute-start | bytes 1376264 | tf_op jit(solution)/shard_map/ppermute | solution.py:28
  921.9 96.6 %collective-permute-start.9 = (bf16[224,1024]{1,0:T(8,128)(2,1)}, bf16[224,1024]{1,0:T(8,128)(2,1)S(1)}, u32[]{:S(2)}, u32[]{:S(2)}) collective-permute-start(bf16[224,1024]{1,0:T(8,128)(2,1)} %bitcast.113), channel_id=1, source_target_pairs={{0,10},{1,11},{2,8},{3,9},{4,14},{5,15},{6,12},{7,13},{8,2},{9,3},... | collective-permute-start | bytes 1376264 | tf_op jit(solution)/shard_map/ppermute | solution.py:28
  934.4 102.0 %collective-permute-start.10 = (bf16[224,1024]{1,0:T(8,128)(2,1)}, bf16[224,1024]{1,0:T(8,128)(2,1)S(1)}, u32[]{:S(2)}, u32[]{:S(2)}) collective-permute-start(bf16[224,1024]{1,0:T(8,128)(2,1)} %bitcast.112), channel_id=1, source_target_pairs={{0,11},{1,10},{2,9},{3,8},{4,15},{5,14},{6,13},{7,12},{8,3},{9,2},... | collective-permute-start | bytes 1376264 | tf_op jit(solution)/shard_map/ppermute | solution.py:28
  943.5 93.8 %collective-permute-start.11 = (bf16[224,1024]{1,0:T(8,128)(2,1)}, bf16[224,1024]{1,0:T(8,128)(2,1)S(1)}, u32[]{:S(2)}, u32[]{:S(2)}) collective-permute-start(bf16[224,1024]{1,0:T(8,128)(2,1)} %bitcast.111), channel_id=1, source_target_pairs={{0,12},{1,13},{2,14},{3,15},{4,8},{5,9},{6,10},{7,11},{8,4},{9,5},... | collective-permute-start | bytes 1376264 | tf_op jit(solution)/shard_map/ppermute | solution.py:28
  984.3 53.8 %collective-permute-start.12 = (bf16[224,1024]{1,0:T(8,128)(2,1)S(1)}, bf16[224,1024]{1,0:T(8,128)(2,1)S(1)}, u32[]{:S(2)}, u32[]{:S(2)}) collective-permute-start(bf16[224,1024]{1,0:T(8,128)(2,1)S(1)} %bitcast.110), channel_id=1, source_target_pairs={{0,13},{1,12},{2,15},{3,14},{4,9},{5,8},{6,11},{7,10},{8,5},{9,4},... | collective-permute-start | bytes 1376264 | tf_op jit(solution)/shard_map/ppermute | solution.py:28
  997.8 41.1 %collective-permute-start.13 = (bf16[224,1024]{1,0:T(8,128)(2,1)S(1)}, bf16[224,1024]{1,0:T(8,128)(2,1)S(1)}, u32[]{:S(2)}, u32[]{:S(2)}) collective-permute-start(bf16[224,1024]{1,0:T(8,128)(2,1)S(1)} %bitcast.109), channel_id=1, source_target_pairs={{0,14},{1,15},{2,12},{3,13},{4,10},{5,11},{6,8},{7,9},{8,6},{9,7},... | collective-permute-start | bytes 1376264 | tf_op jit(solution)/shard_map/ppermute | solution.py:28
  1018.5 21.2 %collective-permute-start.14 = (bf16[224,1024]{1,0:T(8,128)(2,1)S(1)}, bf16[224,1024]{1,0:T(8,128)(2,1)S(1)}, u32[]{:S(2)}, u32[]{:S(2)}) collective-permute-start(bf16[224,1024]{1,0:T(8,128)(2,1)S(1)} %bitcast.108), channel_id=1, source_target_pairs={{0,15},{1,14},{2,13},{3,12},{4,11},{5,10},{6,9},{7,8},{8,7},{9,6},... | collective-permute-start | bytes 1376264 | tf_op jit(solution)/shard_map/ppermute | solution.py:28
  (7 other events, 119.7 us)
Sparse Core Ops, SparseCore 0:
  16.7 180.6 all-gather.2
  220.6 76.7 reduce-scatter.4
  300.1 81.2 all-gather.4
  443.5 206.3 reduce-scatter.6
